TPU v7x, 32 devices: a whole 2x2x4 slice. The times are simulated.
32 devices in a mesh: grp: 2 (over x), tm: 8 (over z, y), inp: 2 (over core).
Axes of the slice: x: 2, y: 2, z: 4, core: 2. Of those that a mesh axis runs over, the one named last changes fastest.
Arguments:
- samples: bfloat16 [256, 1024, 2048], P('grp', ('tm', 'inp')), parts along dimension 0, may hold values from -6 to 6
- filter_taps: float32 [8, 1024], replicated, may hold values from -2 to 2
- flagged: int32 [2048], P('grp'), parts along dimension 0, may hold values 0 or 1
- input_order: int32 [1024], replicated, may hold values from 0 to 1023, each once
Outputs:
- visibilities: bfloat16 [32, 1024, 2048], P(('grp', 'tm'), 'inp'), parts along dimension 0
There are 2 independent parts, one for each index of `grp`. A program takes and returns all parts, laid end to end along the dimension named above; an argument that names none is the same for every part. Nothing has to cross between parts.
Inputs may be any that keep to these rules, and one draw needn't show every extreme that they name: `input_order`: each input appears at exactly one correlator position.
All inputs are finite; a program needn't handle non-finite values.
Results may differ from a plain program's by a relative error of at most 0.007.
Values may be sent and summed in bfloat16 or wider, within the bound.
A program may use at most 128 MiB of HBM per device.

v0:
```python
import math

import jax
import jax.numpy as jnp
from jax import lax
from jax.sharding import PartitionSpec as P

CH_DEV = 2


def dft_table(chan_count, chan_window):
    sample_idx = jnp.arange(chan_count, dtype=jnp.int32)
    channel_idx = jnp.arange(chan_window, dtype=jnp.int32)
    phase_step = sample_idx[:, None] * channel_idx[None, :] % chan_count
    phase_angle = phase_step.astype(jnp.float32) * (2.0 * math.pi / chan_count)
    norm_factor = 1.0 / math.sqrt(chan_count)
    cosine_part = jnp.cos(phase_angle) * norm_factor
    sine_part = jnp.sin(phase_angle) * norm_factor
    upper_rows = jnp.concatenate([cosine_part, -sine_part], axis=1)
    lower_rows = jnp.concatenate([sine_part, cosine_part], axis=1)
    return jnp.concatenate([upper_rows, lower_rows], axis=0)


def shards(samples, filter_taps, flagged, input_order):
    frames_total = samples.shape[0]
    nin_loc = samples.shape[1]
    tap_count = filter_taps.shape[0]
    chan_count = filter_taps.shape[1]
    sections = lax.axis_size("tm")
    groups = lax.axis_size("inp")
    chan_window = CH_DEV * sections
    tap_weights = jnp.concatenate([filter_taps, filter_taps], axis=1)
    transform_table = dft_table(chan_count, chan_window)
    tap_table = (tap_weights[:, :, None] * transform_table[None, :, :]).astype(jnp.bfloat16)
    joined_table = jnp.transpose(tap_table, (1, 0, 2)).reshape(
        2 * chan_count, tap_count * 2 * chan_window
    )
    flat_samples = samples.reshape(frames_total * nin_loc, 2 * chan_count)
    tap_terms = jnp.dot(flat_samples, joined_table, preferred_element_type=jnp.float32)
    tap_terms = tap_terms.reshape(frames_total, nin_loc, tap_count, 2 * chan_window)
    zero_frames = jnp.zeros((tap_count - 1, nin_loc, tap_count, 2 * chan_window), jnp.float32)
    extended = jnp.concatenate([zero_frames, tap_terms], axis=0)
    running = jnp.zeros((frames_total, nin_loc, 2 * chan_window), jnp.float32)
    for tap_index in range(tap_count):
        begin = tap_count - 1 - tap_index
        running = running + extended[begin : begin + frames_total, :, tap_index]
    spectra = jnp.transpose(running.astype(jnp.bfloat16), (2, 0, 1))
    blocks = spectra.reshape(2, sections, CH_DEV, frames_total, nin_loc)
    keep_mask = (1 - flagged).astype(jnp.bfloat16)
    gathered = lax.all_gather(
        lax.all_to_all(blocks, "tm", split_axis=1, concat_axis=4, tiled=True),
        "inp",
        axis=4,
        tiled=True,
    )
    count = gathered.shape[2]
    regrouped = gathered.reshape(2, 1, count, frames_total, groups, sections, nin_loc)
    regrouped = jnp.swapaxes(regrouped, 4, 5).reshape(
        2, count, frames_total, groups * sections * nin_loc
    )
    nin_total = regrouped.shape[3]
    nin_dev = nin_total // groups
    masked = regrouped * keep_mask
    ordered = jnp.take(masked, input_order, axis=3)
    row_block = lax.dynamic_slice_in_dim(ordered, lax.axis_index("inp") * nin_dev, nin_dev, 3)
    real_all = ordered[0]
    imag_all = ordered[1]
    real_rows = row_block[0]
    imag_rows = row_block[1]
    real_vis = jnp.einsum(
        "cfa,cfb->cab", real_rows, real_all, preferred_element_type=jnp.float32
    ) + jnp.einsum("cfa,cfb->cab", imag_rows, imag_all, preferred_element_type=jnp.float32)
    imag_vis = jnp.einsum(
        "cfa,cfb->cab", imag_rows, real_all, preferred_element_type=jnp.float32
    ) - jnp.einsum("cfa,cfb->cab", real_rows, imag_all, preferred_element_type=jnp.float32)
    joined = jnp.concatenate([real_vis, imag_vis], axis=2) * (1.0 / frames_total)
    return joined.astype(jnp.bfloat16)


def solution(mesh):
    placed = (P("grp", ("tm", "inp"), None), P(), P("grp"), P())
    return jax.shard_map(
        shards, mesh=mesh, in_specs=placed, out_specs=P(("grp", "tm"), "inp", None), check_vma=False
    )
```

profile of v0, /device:TPU:1, one launch (start us, length us, event | category | flops | bytes accessed | tf_op | source)
XLA Modules:
  0.0 110.4 jit_solution(7261924167843448848)
XLA Ops:
  6.5 0.0 all-gather.2.cloned.1.call-start
  6.5 0.3 sine_multiply_fusion
  6.8 0.3 fusion.17
  7.1 0.8 maximum_bitcast_fusion
  7.9 0.2 multiply_convert_fusion
  8.1 17.4 %convolution_bitcast_fusion = f32[8192,256]{0,1:T(8,128)} fusion(bf16[2048,256]{0,1:T(8,128)(2,1)S(1)} %bitcast.48, bf16[8192,2048]{1,0:T(8,128)(2,1)} %bitcast.49), kind=kOutput, calls=%fused_computation.8 | convolution fusion | flops 8589934592 | bytes 42991616 | tf_op jit(solution)/shard_map/dot_general | solution.py:39
  25.5 14.2 %reshape.41 = f32[128,64,8,32]{1,0,3,2:T(8,128)} reshape(f32[8192,256]{0,1:T(8,128)} %convolution_bitcast_fusion) | data formatting | bytes 16777216 | tf_op jit(solution)/shard_map/reshape | solution.py:40
  39.7 7.9 %fusion.8 = bf16[128,64,1,32]{1,0,3,2:T(8,128)(2,1)S(1)} fusion(f32[128,64,8,32]{1,0,3,2:T(8,128)} %reshape.41), kind=kLoop, calls=%fused_computation.21 | loop fusion | flops 2097152 | bytes 19398656 | tf_op jit(solution)/shard_map/convert_element_type | solution.py:47
  47.6 0.0 copy-start
  47.6 0.0 copy-start.1
  47.7 0.4 copy.18
  48.1 19.9 %all_to_all.18 = bf16[2,8,2,128,64]{3,4,2,0,1:T(8,128)(2,1)S(1)} all-to-all(bf16[2,8,2,128,64]{3,4,2,0,1:T(8,128)(2,1)S(1)} %copy.18), channel_id=1, replica_groups=mesh['grp'=2,'tm'=8,'inp'=2] {'tm'}, dimensions={1} | all-to-all | bytes 1048576 | tf_op jit(solution)/shard_map/all_to_all | solution.py:51
  67.9 0.8 copy.19
  68.7 0.0 all-gather.2.cloned.1.call-update
  68.8 0.0 copy-done
  68.8 0.0 copy-done.1
  68.8 9.6 %all-gather.2.cloned.1.call-done = bf16[2,1,2,128,1024]{3,4,2,0,1:T(8,128)(2,1)} async-done(((bf16[2,1,2,128,512]{3,4,2,0,1:T(8,128)(2,1)}), bf16[2,1,2,128,1024]{3,4,2,0,1:T(8,128)(2,1)}) %all-gather.2.cloned.1.call-update) | async-done | bytes 1048592 | tf_op jit(solution)/shard_map/all_gather | solution.py:50
  78.5 1.3 %copy.20 = bf16[2,1,2,128,8,2,64]{3,6,5,4,2,0,1:T(8,128)(2,1)S(1)} copy(bf16[2,1,2,128,8,2,64]{3,6,4,5,2,0,1:T(8,128)(2,1)} %bitcast.47) | data formatting | bytes 2097152 | tf_op jit(solution)/shard_map/transpose | solution.py:58
  79.8 11.5 %copy_multiply_fusion = bf16[2,2,128,1024]{2,1,3,0:T(2,128)(2,1)S(1)} fusion(bf16[2,2,128,1024]{2,3,1,0:T(8,128)(2,1)S(1)} %bitcast.45, bf16[1024]{0:T(1024)(128)(2,1)S(1)} %subtract_convert_fusion), kind=kLoop, calls=%fused_computation.22 | loop fusion | flops 524288 | bytes 2099200 | tf_op jit(solution)/shard_map/mul | solution.py:63
  91.3 5.0 %gather_fusion = bf16[1024,2,2,128]{3,2,1,0:T(2,128)(2,1)S(1)} fusion(bf16[2,2,128,1024]{2,1,3,0:T(2,128)(2,1)S(1)} %copy_multiply_fusion, s32[1024]{0:T(1024)S(1)} %fusion.18), kind=kCustom, calls=%fused_computation | custom fusion | bytes 2101248 | tf_op jit(solution)/shard_map/jit(_take)/gather | solution.py:64
  96.3 1.5 %copy.22 = bf16[1024,2,2,128]{0,3,2,1:T(8,128)(2,1)S(1)} copy(bf16[1024,2,2,128]{3,2,1,0:T(2,128)(2,1)S(1)} %gather_fusion) | data formatting | bytes 2097152 | tf_op jit(solution)/shard_map/jit(_take)/gather | solution.py:64
  97.8 0.1 fusion.21
  97.9 0.1 broadcast_select_fusion
  98.0 0.7 fusion.9
  98.8 0.7 fusion.10
  99.5 0.8 convolution_subtract_fusion
  100.3 0.8 convolution_add_fusion
  101.1 2.5 %fusion = bf16[2,512,2048]{2,1,0:T(8,128)(2,1)} fusion(f32[2,512,1024]{2,1,0:T(8,128)S(1)} %convolution_subtract_fusion, f32[2,512,1024]{2,1,0:T(8,128)S(1)} %convolution_add_fusion), kind=kLoop, calls=%fused_computation.10 | loop fusion | flops 6291456 | bytes 12582912 | tf_op jit(solution)/shard_map/convert_element_type | solution.py:77
  (5 shorter events, 0.1 us)
Async XLA Ops:
  6.5 71.9 %all-gather.2.cloned.1.call-start = ((), (), s32[]{:S(2)}) async-start(), calls=%async_computation.1 | async-start | bytes 1572864 | tf_op jit(solution)/shard_map/all_gather | solution.py:50
  47.6 21.1 %copy-start = (s32[1024]{0:T(1024)S(1)}, s32[1024]{0:T(1024)}, u32[]{:S(2)}) copy-start(s32[1024]{0:T(1024)} %param.7) | copy-start | bytes 12292
  47.6 21.2 %copy-start.1 = (s32[1024]{0:T(1024)S(1)}, s32[1024]{0:T(1024)}, u32[]{:S(2)}) copy-start(s32[1024]{0:T(1024)} %param.6) | copy-start | bytes 12292
Sparse Core Ops, SparseCore 0:
  68.9 9.5 all-gather.1
where the time goes:
time: 111 us; the launch traced here: 110 us
  other arithmetic  23.7 us (21%)
  local copies, waits for them, and re-layouts  23.3 us (21%)
  matrix products  20.4 us (18%)
  blocking collectives  19.9 us (18%)
  between operations  13.5 us (12%)
  waiting for transfers between devices  9.66 us (9%)
    all_to_all x1, blocking collectives, shards(): lax.all_to_all(blocks, 'tm', split_axis=1, concat_axis=4, tiled=True)  19.9 us
    dot_general x1, matrix products, shards(): jnp.dot(flat_samples, joined_table, preferred_element_type=jnp.float32)  17.4 us
    reshape x1, local copies, waits for them, and re-layouts, shards(): tap_terms.reshape(frames_total, nin_loc, tap_count, 2 * chan_window)  14.2 us
    mul x1, other arithmetic, shards(): masked = regrouped * keep_mask  11.5 us
    all_gather x1, waiting for transfers between devices, shards(): lax.all_gather(lax.all_to_all(blocks, 'tm', split_axis=1, concat_axis=4,...  9.64 us
    convert_element_type x1, other arithmetic, shards(): spectra = jnp.transpose(running.astype(jnp.bfloat16), (2, 0, 1))  7.93 us
    gather x2, local copies, waits for them, and re-layouts, shards(): ordered = jnp.take(masked, input_order, axis=3)  6.5 us
    convert_element_type x1, other arithmetic, shards(): return joined.astype(jnp.bfloat16)  2.53 us
  transfers between devices with their start and end apart: 1, of which 1 were waited for; matrix products, arithmetic and copies ran while one was open for 0% of the time, Pallas kernels for 0%

commit v1 on v0

v1 whole, which is shorter than its diff:
```python
import functools
import math

import jax
import jax.numpy as jnp
import numpy as np
from jax import lax
from jax.experimental import pallas as pl
from jax.experimental.pallas import tpu as pltpu
from jax.sharding import PartitionSpec as P

LANES = 128
CHUNK_ROWS = 1024
IN_SLOTS = 3
RELAY_LAG = 2
PART_ROWS = 256
VMEM_LIMIT = 48 * 1024 * 1024


def dft_rows(chan_count, sections, chan_dev):
    sample_idx = np.arange(chan_count)
    channel_idx = np.arange(sections * chan_dev)
    angle = (channel_idx[:, None] * sample_idx[None, :] % chan_count) * (2.0 * math.pi / chan_count)
    cosine, sine = np.cos(angle), np.sin(angle)
    real_rows = np.concatenate([cosine, sine], axis=1)
    imag_rows = np.concatenate([-sine, cosine], axis=1)
    rows = np.stack([real_rows, imag_rows], axis=1) / math.sqrt(chan_count)
    return rows.reshape(2 * sections * chan_dev, 2 * chan_count).astype(np.float32)


def filter_kernel(
    chunk_count, sections, samples, taps, dft, gathered,
    inbox, tap_table, terms, wide, outbox, in_sem, send_sem, recv_sem, relay_send, relay_recv,
):
    tap_count, chan_count = taps.shape
    columns = dft.shape[0]
    chunk_frames, nin_loc = inbox.shape[1], inbox.shape[2]
    history = terms.shape[1] - CHUNK_ROWS
    tiles = CHUNK_ROWS // LANES
    me, core = lax.axis_index("tm"), lax.axis_index("inp")

    def fetch(chunk):
        slot = lax.rem(chunk, IN_SLOTS)
        return pltpu.make_async_copy(
            samples.at[pl.ds(chunk * chunk_frames, chunk_frames)], inbox.at[slot], in_sem.at[slot]
        )

    for chunk in range(min(IN_SLOTS, chunk_count)):
        fetch(chunk).start()

    for tap in range(tap_count):
        for half in range(2):
            cols = pl.ds(half * chan_count, chan_count)
            tap_table[pl.ds(tap * columns, columns), cols] = (
                taps[tap : tap + 1, :] * dft[:, cols]
            ).astype(jnp.bfloat16)
    terms[:, :history] = jnp.zeros((terms.shape[0], history), jnp.float32)

    barrier = pltpu.get_barrier_semaphore()

    def greet(step, carry):
        pl.semaphore_signal(
            barrier, inc=1, device_id={"tm": lax.rem(me + step, sections)},
            device_id_type=pl.DeviceIdType.MESH,
        )
        return carry

    lax.fori_loop(1, sections, greet, 0)
    pl.semaphore_signal(
        barrier, inc=1, device_id={"inp": 1 - core}, device_id_type=pl.DeviceIdType.MESH
    )
    pl.semaphore_wait(barrier, sections)

    def message(chunk, step):
        owner = lax.rem(me + step, sections)
        return pltpu.make_async_remote_copy(
            src_ref=outbox.at[chunk, owner],
            dst_ref=gathered.at[core, chunk, me],
            send_sem=send_sem.at[chunk, step],
            recv_sem=recv_sem.at[chunk, me],
            device_id={"tm": owner},
            device_id_type=pl.DeviceIdType.MESH,
        )

    def arrival(chunk, step):
        source = lax.rem(me + step, sections)
        return pltpu.make_async_remote_copy(
            src_ref=outbox.at[chunk, source],
            dst_ref=gathered.at[core, chunk, source],
            send_sem=send_sem.at[chunk, step],
            recv_sem=recv_sem.at[chunk, source],
            device_id={"tm": source},
            device_id_type=pl.DeviceIdType.MESH,
        )

    def relay(chunk, half):
        return pltpu.make_async_remote_copy(
            src_ref=gathered.at[half, chunk],
            dst_ref=gathered.at[half, chunk],
            send_sem=relay_send.at[chunk],
            recv_sem=relay_recv.at[chunk],
            device_id={"inp": 1 - core},
            device_id_type=pl.DeviceIdType.MESH,
        )

    def pass_on(chunk):
        def take(step, carry):
            arrival(chunk, step).wait_recv()
            return carry

        lax.fori_loop(1, sections, take, 0)
        relay(chunk, core).start()

    def one_chunk(chunk, carry):
        fetch(chunk).wait()
        slot = lax.rem(chunk, IN_SLOTS)
        part_frames = PART_ROWS // nin_loc
        for part in range(CHUNK_ROWS // PART_ROWS):
            block = inbox[slot, pl.ds(part * part_frames, part_frames)]
            terms[:, pl.ds(history + part * PART_ROWS, PART_ROWS)] = lax.dot_general(
                tap_table[...], block.reshape(PART_ROWS, 2 * chan_count),
                (((1,), (1,)), ((), ())), preferred_element_type=jnp.float32,
            )

        @pl.when(chunk + IN_SLOTS < chunk_count)
        def _():
            fetch(chunk + IN_SLOTS).start()

        total = None
        for rest in range(0, LANES, nin_loc):
            held = None
            for tap in range(tap_count):
                if tap * nin_loc % LANES != rest:
                    continue
                lead = LANES if rest else 0
                start = history - (tap * nin_loc - rest) - lead
                piece = terms[pl.ds(tap * columns, columns), pl.ds(start, CHUNK_ROWS + lead)]
                held = piece if held is None else held + piece
            if held is None:
                continue
            if rest:
                held = pltpu.roll(held, rest, 1)[:, LANES:]
            total = held if total is None else total + held
        terms[:, :history] = terms[:, CHUNK_ROWS:]
        for tile in range(tiles):
            wide[pl.ds(tile, columns, stride=tiles), :] = total[:, tile * LANES : (tile + 1) * LANES]
        outbox[chunk] = wide[...].astype(jnp.bfloat16).reshape(outbox.shape[1:])
        gathered[core, chunk, me] = outbox[chunk, me]

        def send(step, carry):
            message(chunk, step).start()
            return carry

        lax.fori_loop(1, sections, send, 0)

        @pl.when(chunk >= RELAY_LAG)
        def _():
            pass_on(chunk - RELAY_LAG)

        return carry

    lax.fori_loop(0, chunk_count, one_chunk, 0)

    def late(chunk, carry):
        pass_on(chunk)
        return carry

    lax.fori_loop(max(chunk_count - RELAY_LAG, 0), chunk_count, late, 0)

    def finish(chunk, carry):
        def sent(step, inner):
            message(chunk, step).wait_send()
            return inner

        lax.fori_loop(1, sections, sent, 0)
        relay(chunk, core).wait_send()
        relay(chunk, 1 - core).wait_recv()
        return carry

    lax.fori_loop(0, chunk_count, finish, 0)


def correlate_kernel(
    frames_total, nin_loc, gathered, flagged, order, out, onehot, turned, plain, result, out_sem
):
    chunk_count = gathered.shape[1]
    chan_dev, nin_dev, width = out.shape
    nin_total = width // 2
    pack = LANES // nin_loc
    half_rows = gathered.shape[3] // chan_dev
    depth = pack * chunk_count * half_rows
    first = pl.multiple_of(lax.axis_index("inp") * nin_dev, LANES)
    keep = (1 - flagged[...]).astype(jnp.float32).astype(jnp.bfloat16)
    step = 256
    for base in range(0, nin_total, step):
        index = lax.broadcasted_iota(jnp.int32, (step, nin_total), 0) + base
        onehot[pl.ds(base, step), :] = jnp.where(order[...] == index, 1.0, 0.0).astype(jnp.bfloat16)

    copies = []
    for chan in range(chan_dev):
        rows = pl.ds(chan * half_rows, half_rows)
        groups = []
        for lane in range(pack):
            blocks = []
            for block in range(nin_total // LANES):
                pieces = []
                for source in range(block * pack, (block + 1) * pack):
                    piece = gathered[source % 2, :, source // 2, rows, :]
                    piece = piece.reshape(chunk_count * half_rows, LANES)
                    pieces.append(piece[:, lane * nin_loc : (lane + 1) * nin_loc])
                blocks.append(jnp.concatenate(pieces, axis=1))
            groups.append(jnp.concatenate(blocks, axis=1))
        inputs = jnp.concatenate(groups, axis=0) * keep
        placed = jnp.dot(inputs, onehot[...], preferred_element_type=jnp.float32)
        plain[chan] = placed.astype(jnp.bfloat16)
        split = placed.reshape(depth // half_rows, 2, half_rows // 2, nin_total)
        swapped = jnp.stack([split[:, 1], -split[:, 0]], axis=1)
        turned[chan] = swapped.reshape(depth, nin_total).astype(jnp.bfloat16)
        for part, source in enumerate((plain, turned)):
            product = lax.dot_general(
                source[chan, :, pl.ds(first, nin_dev)], plain[chan],
                (((0,), (0,)), ((), ())), preferred_element_type=jnp.float32,
            )
            columns = pl.ds(part * nin_total, nin_total)
            result[chan, :, columns] = (product * (1.0 / frames_total)).astype(jnp.bfloat16)
            copy = pltpu.make_async_copy(
                result.at[chan, :, columns], out.at[chan, :, columns], out_sem.at[chan, part]
            )
            copy.start()
            copies.append(copy)
    for copy in copies:
        copy.wait()


def shards(chan_dev, sections, samples, filter_taps, flagged, input_order):
    frames_total, nin_loc, width = samples.shape
    tap_count, chan_count = filter_taps.shape
    nin_total = input_order.shape[0]
    columns = 2 * sections * chan_dev
    chunk_frames = CHUNK_ROWS // nin_loc
    chunk_count = frames_total // chunk_frames
    tiles = CHUNK_ROWS // LANES
    history = -(-(tap_count - 1) * nin_loc // LANES) * LANES
    rows = 2 * chan_dev * tiles
    vmem = pl.BlockSpec(memory_space=pltpu.VMEM)
    hbm = pl.BlockSpec(memory_space=pl.ANY)

    gathered = pl.pallas_call(
        functools.partial(filter_kernel, chunk_count, sections),
        out_shape=jax.ShapeDtypeStruct((2, chunk_count, sections, rows, LANES), jnp.bfloat16),
        in_specs=[hbm, vmem, vmem],
        out_specs=vmem,
        scratch_shapes=[
            pltpu.VMEM((IN_SLOTS, chunk_frames, nin_loc, width), jnp.bfloat16),
            pltpu.VMEM((tap_count * columns, width), jnp.bfloat16),
            pltpu.VMEM((tap_count * columns, history + CHUNK_ROWS), jnp.float32),
            pltpu.VMEM((columns * tiles, LANES), jnp.float32),
            pltpu.VMEM((chunk_count, sections, rows, LANES), jnp.bfloat16),
            pltpu.SemaphoreType.DMA((IN_SLOTS,)),
            pltpu.SemaphoreType.DMA((chunk_count, sections)),
            pltpu.SemaphoreType.DMA((chunk_count, sections)),
            pltpu.SemaphoreType.DMA((chunk_count,)),
            pltpu.SemaphoreType.DMA((chunk_count,)),
        ],
        compiler_params=pltpu.CompilerParams(
            collective_id=0, has_side_effects=True, vmem_limit_bytes=VMEM_LIMIT
        ),
        name="filter_exchange",
    )(samples, filter_taps, jnp.asarray(dft_rows(chan_count, sections, chan_dev)))

    nin_dev = nin_total // 2
    depth = 2 * frames_total
    return pl.pallas_call(
        functools.partial(correlate_kernel, frames_total, nin_loc),
        out_shape=jax.ShapeDtypeStruct((chan_dev, nin_dev, 2 * nin_total), jnp.bfloat16),
        in_specs=[vmem, vmem, vmem],
        out_specs=hbm,
        scratch_shapes=[
            pltpu.VMEM((nin_total, nin_total), jnp.bfloat16),
            pltpu.VMEM((chan_dev, depth, nin_total), jnp.bfloat16),
            pltpu.VMEM((chan_dev, depth, nin_total), jnp.bfloat16),
            pltpu.VMEM((chan_dev, nin_dev, 2 * nin_total), jnp.bfloat16),
            pltpu.SemaphoreType.DMA((chan_dev, 2)),
        ],
        compiler_params=pltpu.CompilerParams(vmem_limit_bytes=VMEM_LIMIT),
        name="correlate",
    )(gathered, flagged.reshape(1, nin_total), input_order.reshape(1, nin_total))


def solution(mesh):
    placed = (P("grp", ("tm", "inp"), None), P(), P("grp"), P())
    return jax.shard_map(
        functools.partial(shards, 2, mesh.shape["tm"]),
        mesh=mesh,
        in_specs=placed,
        out_specs=P(("grp", "tm"), "inp", None),
        check_vma=False,
    )
```

time: 111 us -> 32.6 us (0.29)
  Pallas kernels: 0 us -> 30.6 us
  other arithmetic: 23.7 us -> 0 us
  local copies, waits for them, and re-layouts: 23.3 us -> 1.71 us
  matrix products: 20.4 us -> 0 us
  blocking collectives: 19.9 us -> 0 us
  between operations: 13.5 us -> 0.03 us
  waiting for transfers between devices: 9.66 us -> 0 us
    pallas_call x0 -> x2, Pallas kernels: none -> 30.6 us  [the longest x1 26.5 us: shards(): pl.pallas_call(functools.partial(filter_kernel, chunk_count, sections), o...]
    dot_general x5 -> x0, matrix products: 20.4 us -> none  [the longest x1 17.4 us: shards(): jnp.dot(flat_samples, joined_table, preferred_element_type=jnp.float32)]
    all_to_all x1 -> x0, blocking collectives: 19.9 us -> none  [shards(): lax.all_to_all(blocks, 'tm', split_axis=1, concat_axis=4, tiled=True)]
    reshape x2 -> x0, local copies, waits for them, and re-layouts: 14.6 us -> none  [the longest x1 14.2 us: shards(): tap_terms.reshape(frames_total, nin_loc, tap_count, 2 * chan_window)]
    mul x3 -> x0, other arithmetic: 12.6 us -> none  [the longest x1 11.5 us: shards(): masked = regrouped * keep_mask]
    convert_element_type x4 -> x0, other arithmetic: 10.6 us -> none  [the longest x1 7.93 us: shards(): spectra = jnp.transpose(running.astype(jnp.bfloat16), (2, 0, 1))]
    all_gather x1 -> x0, waiting for transfers between devices: 9.64 us -> none  [shards(): lax.all_gather(lax.all_to_all(blocks, 'tm', split_axis=1, concat_axis=4,...]
    gather x2 -> x0, local copies, waits for them, and re-layouts: 6.5 us -> none  [shards(): ordered = jnp.take(masked, input_order, axis=3)]
  transfers between devices with their start and end apart: 1 -> 0, of which waited for: 1 -> 0; matrix products, arithmetic and copies ran while one was open for 0% -> 0% of each run, Pallas kernels for 0% -> 0%
where the time goes in v1:
time: 32.6 us; the launch traced here: 32.3 us
  Pallas kernels  30.6 us (94%)
  local copies, waits for them, and re-layouts  1.71 us (5%)
    pallas_call x1, Pallas kernels, shards(): pl.pallas_call(functools.partial(filter_kernel, chunk_count, sections), o...  26.5 us
    pallas_call x1, Pallas kernels, shards(): pl.pallas_call(functools.partial(correlate_kernel, frames_total, nin_loc)...  4.03 us
    unnamed x8, local copies, waits for them, and re-layouts  1.71 us

profile of v1, /device:TPU:1, one launch (start us, length us, event | category | flops | bytes accessed | tf_op | source)
XLA Modules:
  0.0 32.3 jit_solution(9506755596981856714)
XLA Ops:
  0.0 0.0 copy-start
  0.0 0.9 %copy-done = f32[32,2048]{1,0:T(8,128)S(1)} copy-done((f32[32,2048]{1,0:T(8,128)S(1)}, f32[32,2048]{1,0:T(8,128)}, u32[]{:S(2)}) %copy-start) | copy-done | bytes 262168
  1.0 0.0 copy-start.1
  1.0 0.8 %copy-done.1 = f32[8,1024]{1,0:T(8,128)S(1)} copy-done((f32[8,1024]{1,0:T(8,128)S(1)}, f32[8,1024]{1,0:T(8,128)}, u32[]{:S(2)}) %copy-start.1) | copy-done | bytes 32792
  1.7 0.0 copy-start.2
  1.7 0.0 copy-start.3
  1.7 26.5 %filter_exchange.1.gathered = bf16[2,8,8,32,128]{4,3,2,1,0:T(8,128)(2,1)S(1)} custom-call(bf16[128,64,2048]{2,1,0:T(8,128)(2,1)} %samples.1, f32[8,1024]{1,0:T(8,128)S(1)} %copy-done.1, f32[32,2048]{1,0:T(8,128)S(1)} %copy-done), custom_call_target="tpu_custom_call" | custom-call | tf_op jit(solution)/shard_map/filter_exchange/pallas_call | solution.py:248
  28.3 0.0 copy-done.2
  28.3 0.0 copy-done.3
  28.3 4.0 %correlate.1 = bf16[2,512,2048]{2,1,0:T(8,128)(2,1)} custom-call(bf16[2,8,8,32,128]{4,3,2,1,0:T(8,128)(2,1)S(1)} %filter_exchange.1.gathered, s32[1,1024]{1,0:T(1,128)S(1)} %bitcast.2, s32[1,1024]{1,0:T(1,128)S(1)} %bitcast.3), custom_call_target="tpu_custom_call" | custom-call | tf_op jit(solution)/shard_map/correlate/pallas_call | solution.py:273
Async XLA Ops:
  0.0 0.9 %copy-start = (f32[32,2048]{1,0:T(8,128)S(1)}, f32[32,2048]{1,0:T(8,128)}, u32[]{:S(2)}) copy-start(f32[32,2048]{1,0:T(8,128)} %constant.2.clone.dft) | copy-start | bytes 786436
  1.0 0.8 %copy-start.1 = (f32[8,1024]{1,0:T(8,128)S(1)}, f32[8,1024]{1,0:T(8,128)}, u32[]{:S(2)}) copy-start(f32[8,1024]{1,0:T(8,128)} %taps.1) | copy-start | bytes 98308
  1.7 26.6 %copy-start.2 = (s32[1024]{0:T(1024)S(1)}, s32[1024]{0:T(1024)}, u32[]{:S(2)}) copy-start(s32[1024]{0:T(1024)} %param.7) | copy-start | bytes 12292
  1.7 26.6 %copy-start.3 = (s32[1024]{0:T(1024)S(1)}, s32[1024]{0:T(1024)}, u32[]{:S(2)}) copy-start(s32[1024]{0:T(1024)} %param.8) | copy-start | bytes 12292

commit v2 on v1

--- a/solution.py
+++ b/solution.py
@@ -12,7 +12,7 @@
 LANES = 128
 CHUNK_ROWS = 1024
 IN_SLOTS = 3
-RELAY_LAG = 2
+RELAY_LAG = 4
 PART_ROWS = 256
 VMEM_LIMIT = 48 * 1024 * 1024
 
@@ -29,25 +29,59 @@
 
 
 def filter_kernel(
-    chunk_count, sections, samples, taps, dft, gathered,
-    inbox, tap_table, terms, wide, outbox, in_sem, send_sem, recv_sem, relay_send, relay_recv,
+    chunk_count, sections, samples, taps_in, dft_in, flagged_in, order_in, plain, turned,
+    taps, dft, flagged, order, onehot, gathered, inbox, tap_table, terms, wide, outbox,
+    small_sem, in_sem, send_sem, recv_sem, relay_send, relay_recv,
 ):
     tap_count, chan_count = taps.shape
     columns = dft.shape[0]
     chunk_frames, nin_loc = inbox.shape[1], inbox.shape[2]
     history = terms.shape[1] - CHUNK_ROWS
     tiles = CHUNK_ROWS // LANES
+    parts = CHUNK_ROWS // PART_ROWS
+    part_frames = PART_ROWS // nin_loc
+    nin_total = order.shape[1]
+    chan_dev = plain.shape[0]
+    pack = LANES // nin_loc
     me, core = lax.axis_index("tm"), lax.axis_index("inp")
 
-    def fetch(chunk):
+    small = [
+        pltpu.make_async_copy(source, target, small_sem.at[index])
+        for index, (source, target) in enumerate(
+            ((taps_in, taps), (dft_in, dft), (flagged_in, flagged), (order_in, order))
+        )
+    ]
+    for copy in small:
+        copy.start()
+
+    def fetch(chunk, part):
         slot = lax.rem(chunk, IN_SLOTS)
         return pltpu.make_async_copy(
-            samples.at[pl.ds(chunk * chunk_frames, chunk_frames)], inbox.at[slot], in_sem.at[slot]
+            samples.at[pl.ds(chunk * chunk_frames + part * part_frames, part_frames)],
+            inbox.at[slot, pl.ds(part * part_frames, part_frames)],
+            in_sem.at[slot, part],
         )
 
     for chunk in range(min(IN_SLOTS, chunk_count)):
-        fetch(chunk).start()
-
+        for part in range(parts):
+            fetch(chunk, part).start()
+
+    barrier = pltpu.get_barrier_semaphore()
+
+    def greet(step, carry):
+        pl.semaphore_signal(
+            barrier, inc=1, device_id={"tm": lax.rem(me + step, sections)},
+            device_id_type=pl.DeviceIdType.MESH,
+        )
+        return carry
+
+    lax.fori_loop(1, sections, greet, 0)
+    pl.semaphore_signal(
+        barrier, inc=1, device_id={"inp": 1 - core}, device_id_type=pl.DeviceIdType.MESH
+    )
+
+    for copy in small:
+        copy.wait()
     for tap in range(tap_count):
         for half in range(2):
             cols = pl.ds(half * chan_count, chan_count)
@@ -56,20 +90,13 @@
             ).astype(jnp.bfloat16)
     terms[:, :history] = jnp.zeros((terms.shape[0], history), jnp.float32)
 
-    barrier = pltpu.get_barrier_semaphore()
-
-    def greet(step, carry):
-        pl.semaphore_signal(
-            barrier, inc=1, device_id={"tm": lax.rem(me + step, sections)},
-            device_id_type=pl.DeviceIdType.MESH,
+    def mark(base, carry):
+        start = pl.multiple_of(base * PART_ROWS, PART_ROWS)
+        index = lax.broadcasted_iota(jnp.int32, (PART_ROWS, nin_total), 0) + start
+        onehot[pl.ds(start, PART_ROWS), :] = jnp.where(order[...] == index, 1.0, 0.0).astype(
+            jnp.bfloat16
         )
         return carry
-
-    lax.fori_loop(1, sections, greet, 0)
-    pl.semaphore_signal(
-        barrier, inc=1, device_id={"inp": 1 - core}, device_id_type=pl.DeviceIdType.MESH
-    )
-    pl.semaphore_wait(barrier, sections)
 
     def message(chunk, step):
         owner = lax.rem(me + step, sections)
@@ -112,10 +139,9 @@
         relay(chunk, core).start()
 
     def one_chunk(chunk, carry):
-        fetch(chunk).wait()
         slot = lax.rem(chunk, IN_SLOTS)
-        part_frames = PART_ROWS // nin_loc
-        for part in range(CHUNK_ROWS // PART_ROWS):
+        for part in range(parts):
+            fetch(chunk, part).wait()
             block = inbox[slot, pl.ds(part * part_frames, part_frames)]
             terms[:, pl.ds(history + part * PART_ROWS, PART_ROWS)] = lax.dot_general(
                 tap_table[...], block.reshape(PART_ROWS, 2 * chan_count),
@@ -124,7 +150,8 @@
 
         @pl.when(chunk + IN_SLOTS < chunk_count)
         def _():
-            fetch(chunk + IN_SLOTS).start()
+            for part in range(parts):
+                fetch(chunk + IN_SLOTS, part).start()
 
         total = None
         for rest in range(0, LANES, nin_loc):
@@ -147,6 +174,11 @@
         outbox[chunk] = wide[...].astype(jnp.bfloat16).reshape(outbox.shape[1:])
         gathered[core, chunk, me] = outbox[chunk, me]
 
+        @pl.when(chunk == 0)
+        def _():
+            lax.fori_loop(0, nin_total // PART_ROWS, mark, 0)
+            pl.semaphore_wait(barrier, sections)
+
         def send(step, carry):
             message(chunk, step).start()
             return carry
@@ -161,61 +193,65 @@
 
     lax.fori_loop(0, chunk_count, one_chunk, 0)
 
-    def late(chunk, carry):
-        pass_on(chunk)
-        return carry
-
-    lax.fori_loop(max(chunk_count - RELAY_LAG, 0), chunk_count, late, 0)
-
-    def finish(chunk, carry):
-        def sent(step, inner):
-            message(chunk, step).wait_send()
-            return inner
-
-        lax.fori_loop(1, sections, sent, 0)
-        relay(chunk, core).wait_send()
-        relay(chunk, 1 - core).wait_recv()
-        return carry
-
-    lax.fori_loop(0, chunk_count, finish, 0)
-
-
-def correlate_kernel(
-    frames_total, nin_loc, gathered, flagged, order, out, onehot, turned, plain, result, out_sem
-):
-    chunk_count = gathered.shape[1]
-    chan_dev, nin_dev, width = out.shape
-    nin_total = width // 2
-    pack = LANES // nin_loc
+    keep = (1 - flagged[...]).astype(jnp.float32).astype(jnp.bfloat16)
+    batch = max(chunk_count // 2, 1)
     half_rows = gathered.shape[3] // chan_dev
-    depth = pack * chunk_count * half_rows
-    first = pl.multiple_of(lax.axis_index("inp") * nin_dev, LANES)
-    keep = (1 - flagged[...]).astype(jnp.float32).astype(jnp.bfloat16)
-    step = 256
-    for base in range(0, nin_total, step):
-        index = lax.broadcasted_iota(jnp.int32, (step, nin_total), 0) + base
-        onehot[pl.ds(base, step), :] = jnp.where(order[...] == index, 1.0, 0.0).astype(jnp.bfloat16)
-
-    copies = []
-    for chan in range(chan_dev):
-        rows = pl.ds(chan * half_rows, half_rows)
+    batch_rows = pack * batch * half_rows
+
+    def place(begin):
+        for chunk in range(begin, begin + batch):
+            relay(chunk, 1 - core).wait_recv()
         groups = []
         for lane in range(pack):
             blocks = []
             for block in range(nin_total // LANES):
                 pieces = []
                 for source in range(block * pack, (block + 1) * pack):
-                    piece = gathered[source % 2, :, source // 2, rows, :]
-                    piece = piece.reshape(chunk_count * half_rows, LANES)
+                    piece = gathered[source % 2, begin : begin + batch, source // 2]
+                    piece = piece.reshape(batch * chan_dev * half_rows, LANES)
                     pieces.append(piece[:, lane * nin_loc : (lane + 1) * nin_loc])
                 blocks.append(jnp.concatenate(pieces, axis=1))
             groups.append(jnp.concatenate(blocks, axis=1))
         inputs = jnp.concatenate(groups, axis=0) * keep
         placed = jnp.dot(inputs, onehot[...], preferred_element_type=jnp.float32)
-        plain[chan] = placed.astype(jnp.bfloat16)
-        split = placed.reshape(depth // half_rows, 2, half_rows // 2, nin_total)
-        swapped = jnp.stack([split[:, 1], -split[:, 0]], axis=1)
-        turned[chan] = swapped.reshape(depth, nin_total).astype(jnp.bfloat16)
+        split = placed.reshape(pack * batch, chan_dev, 2, half_rows // 2, nin_total)
+        swapped = jnp.stack([split[:, :, 1], -split[:, :, 0]], axis=2)
+        rows = pl.ds(begin // batch * batch_rows, batch_rows)
+        for chan in range(chan_dev):
+            plain[chan, rows, :] = (
+                split[:, chan].reshape(batch_rows, nin_total).astype(jnp.bfloat16)
+            )
+            turned[chan, rows, :] = (
+                swapped[:, chan].reshape(batch_rows, nin_total).astype(jnp.bfloat16)
+            )
+
+    late = range(max(chunk_count - RELAY_LAG, 0), chunk_count)
+    for chunk in late[: len(late) // 2]:
+        pass_on(chunk)
+    place(0)
+    for chunk in late[len(late) // 2 :]:
+        pass_on(chunk)
+    for begin in range(batch, chunk_count, batch):
+        place(begin)
+
+    def finish(chunk, carry):
+        def sent(step, inner):
+            message(chunk, step).wait_send()
+            return inner
+
+        lax.fori_loop(1, sections, sent, 0)
+        relay(chunk, core).wait_send()
+        return carry
+
+    lax.fori_loop(0, chunk_count, finish, 0)
+
+
+def correlate_kernel(frames_total, plain, turned, out, result, out_sem):
+    chan_dev, nin_dev, width = out.shape
+    nin_total = width // 2
+    first = pl.multiple_of(lax.axis_index("inp") * nin_dev, LANES)
+    copies = []
+    for chan in range(chan_dev):
         for part, source in enumerate((plain, turned)):
             product = lax.dot_general(
                 source[chan, :, pl.ds(first, nin_dev)], plain[chan],
@@ -243,20 +279,31 @@
     history = -(-(tap_count - 1) * nin_loc // LANES) * LANES
     rows = 2 * chan_dev * tiles
     vmem = pl.BlockSpec(memory_space=pltpu.VMEM)
-    hbm = pl.BlockSpec(memory_space=pl.ANY)
-
-    gathered = pl.pallas_call(
+
+    hbm = pl.BlockSpec(memory_space=pltpu.HBM)
+    nin_dev = nin_total // 2
+    depth = 2 * frames_total
+    placed = jax.ShapeDtypeStruct((chan_dev, depth, nin_total), jnp.bfloat16)
+
+    plain, turned = pl.pallas_call(
         functools.partial(filter_kernel, chunk_count, sections),
-        out_shape=jax.ShapeDtypeStruct((2, chunk_count, sections, rows, LANES), jnp.bfloat16),
-        in_specs=[hbm, vmem, vmem],
-        out_specs=vmem,
+        out_shape=(placed, placed),
+        in_specs=[hbm] * 5,
+        out_specs=(vmem, vmem),
         scratch_shapes=[
+            pltpu.VMEM((tap_count, chan_count), jnp.float32),
+            pltpu.VMEM((columns, width), jnp.float32),
+            pltpu.VMEM((1, nin_total), jnp.int32),
+            pltpu.VMEM((1, nin_total), jnp.int32),
+            pltpu.VMEM((nin_total, nin_total), jnp.bfloat16),
+            pltpu.VMEM((2, chunk_count, sections, rows, LANES), jnp.bfloat16),
             pltpu.VMEM((IN_SLOTS, chunk_frames, nin_loc, width), jnp.bfloat16),
             pltpu.VMEM((tap_count * columns, width), jnp.bfloat16),
             pltpu.VMEM((tap_count * columns, history + CHUNK_ROWS), jnp.float32),
             pltpu.VMEM((columns * tiles, LANES), jnp.float32),
             pltpu.VMEM((chunk_count, sections, rows, LANES), jnp.bfloat16),
-            pltpu.SemaphoreType.DMA((IN_SLOTS,)),
+            pltpu.SemaphoreType.DMA((4,)),
+            pltpu.SemaphoreType.DMA((IN_SLOTS, CHUNK_ROWS // PART_ROWS)),
             pltpu.SemaphoreType.DMA((chunk_count, sections)),
             pltpu.SemaphoreType.DMA((chunk_count, sections)),
             pltpu.SemaphoreType.DMA((chunk_count,)),
@@ -266,25 +313,29 @@
             collective_id=0, has_side_effects=True, vmem_limit_bytes=VMEM_LIMIT
         ),
         name="filter_exchange",
-    )(samples, filter_taps, jnp.asarray(dft_rows(chan_count, sections, chan_dev)))
-
-    nin_dev = nin_total // 2
-    depth = 2 * frames_total
+    )(
+        samples,
+        *(
+            pltpu.with_memory_space_constraint(operand, pltpu.HBM)
+            for operand in (
+                filter_taps, jnp.asarray(dft_rows(chan_count, sections, chan_dev)),
+                flagged.reshape(1, nin_total), input_order.reshape(1, nin_total),
+            )
+        ),
+    )
+
     return pl.pallas_call(
-        functools.partial(correlate_kernel, frames_total, nin_loc),
+        functools.partial(correlate_kernel, frames_total),
         out_shape=jax.ShapeDtypeStruct((chan_dev, nin_dev, 2 * nin_total), jnp.bfloat16),
-        in_specs=[vmem, vmem, vmem],
+        in_specs=[vmem, vmem],
         out_specs=hbm,
         scratch_shapes=[
-            pltpu.VMEM((nin_total, nin_total), jnp.bfloat16),
-            pltpu.VMEM((chan_dev, depth, nin_total), jnp.bfloat16),
-            pltpu.VMEM((chan_dev, depth, nin_total), jnp.bfloat16),
             pltpu.VMEM((chan_dev, nin_dev, 2 * nin_total), jnp.bfloat16),
             pltpu.SemaphoreType.DMA((chan_dev, 2)),
         ],
         compiler_params=pltpu.CompilerParams(vmem_limit_bytes=VMEM_LIMIT),
         name="correlate",
-    )(gathered, flagged.reshape(1, nin_total), input_order.reshape(1, nin_total))
+    )(plain, turned)
 
 
 def solution(mesh):

time: 32.6 us -> 43.1 us (1.32)
  Pallas kernels: 30.6 us -> 43 us
  local copies, waits for them, and re-layouts: 1.71 us -> 0 us
    pallas_call x1, Pallas kernels: 26.5 us -> 40.5 us  [shards(): pl.pallas_call(functools.partial(filter_kernel, chunk_count, sections), o...]
    unnamed x8 -> x0, local copies, waits for them, and re-layouts: 1.71 us -> none
    pallas_call x1, Pallas kernels: 4.03 us -> 2.52 us  [shards(): pl.pallas_call(functools.partial(correlate_kernel, frames_total), out_sha...]
where the time goes in v2:
time: 43.1 us; the launch traced here: 43 us
  Pallas kernels  43 us (100%)
    pallas_call x1, Pallas kernels, shards(): pl.pallas_call(functools.partial(filter_kernel, chunk_count, sections), o...  40.5 us
    pallas_call x1, Pallas kernels, shards(): pl.pallas_call(functools.partial(correlate_kernel, frames_total), out_sha...  2.52 us

profile of v2, /device:TPU:1, one launch (start us, length us, event | category | flops | bytes accessed | tf_op | source)
XLA Modules:
  0.0 43.0 jit_solution(5969275016482714607)
XLA Ops:
  0.0 40.5 %filter_exchange.1 = (bf16[2,256,1024]{2,1,0:T(8,128)(2,1)S(1)}, bf16[2,256,1024]{2,1,0:T(8,128)(2,1)S(1)}) custom-call(bf16[128,64,2048]{2,1,0:T(8,128)(2,1)} %samples.1, f32[8,1024]{1,0:T(8,128)} %taps_in.1, f32[32,2048]{1,0:T(8,128)} %constant.2.clone.dft_in, s32[1,1024]{1,0:T(1,128)} %bitcast.2, s32[1,1024]{1,0:T(1,128)} %bitcast.3), custom_call_target="tpu_custom_call" | custom-call | tf_op jit(solution)/shard_map/filter_exchange/pallas_call | solution.py:288
  40.5 2.5 %correlate.1 = bf16[2,512,2048]{2,1,0:T(8,128)(2,1)} custom-call(bf16[2,256,1024]{2,1,0:T(8,128)(2,1)S(1)} %get-tuple-element.7.plain, bf16[2,256,1024]{2,1,0:T(8,128)(2,1)S(1)} %get-tuple-element.8.turned), custom_call_target="tpu_custom_call" | custom-call | tf_op jit(solution)/shard_map/correlate/pallas_call | solution.py:327

commit v3 on v2

--- a/solution.py
+++ b/solution.py
@@ -13,7 +13,7 @@
 CHUNK_ROWS = 1024
 IN_SLOTS = 3
 RELAY_LAG = 4
-PART_ROWS = 256
+PART_ROWS = 1024
 VMEM_LIMIT = 48 * 1024 * 1024
 
 

time: 43.1 us -> 29.4 us (0.68)
  Pallas kernels: 43 us -> 29.3 us
    pallas_call x1, Pallas kernels: 40.5 us -> 26.8 us  [shards(): pl.pallas_call(functools.partial(filter_kernel, chunk_count, sections), o...]
where the time goes in v3:
time: 29.4 us; the launch traced here: 29.3 us
  Pallas kernels  29.3 us (100%)
    pallas_call x1, Pallas kernels, shards(): pl.pallas_call(functools.partial(filter_kernel, chunk_count, sections), o...  26.8 us
    pallas_call x1, Pallas kernels, shards(): pl.pallas_call(functools.partial(correlate_kernel, frames_total), out_sha...  2.52 us

profile of v3, /device:TPU:1, one launch (start us, length us, event | category | flops | bytes accessed | tf_op | source)
XLA Modules:
  0.0 29.3 jit_solution(13787747735178385986)
XLA Ops:
  0.0 26.8 %filter_exchange.1 = (bf16[2,256,1024]{2,1,0:T(8,128)(2,1)S(1)}, bf16[2,256,1024]{2,1,0:T(8,128)(2,1)S(1)}) custom-call(bf16[128,64,2048]{2,1,0:T(8,128)(2,1)} %samples.1, f32[8,1024]{1,0:T(8,128)} %taps_in.1, f32[32,2048]{1,0:T(8,128)} %constant.2.clone.dft_in, s32[1,1024]{1,0:T(1,128)} %bitcast.2, s32[1,1024]{1,0:T(1,128)} %bitcast.3), custom_call_target="tpu_custom_call" | custom-call | tf_op jit(solution)/shard_map/filter_exchange/pallas_call | solution.py:288
  26.8 2.5 %correlate.1 = bf16[2,512,2048]{2,1,0:T(8,128)(2,1)} custom-call(bf16[2,256,1024]{2,1,0:T(8,128)(2,1)S(1)} %get-tuple-element.7.plain, bf16[2,256,1024]{2,1,0:T(8,128)(2,1)S(1)} %get-tuple-element.8.turned), custom_call_target="tpu_custom_call" | custom-call | tf_op jit(solution)/shard_map/correlate/pallas_call | solution.py:327
